TPU v7x, 32 devices: a whole 2x2x4 slice. The times are simulated.
32 devices in a mesh: face: 4 (over y, x), elem: 8 (over z, core).
Axes of the slice: x: 2, y: 2, z: 4, core: 2. Of those that a mesh axis runs over, the one named last changes fastest.
Arguments:
- field_state: float32 [432, 16384], P(None, ('face', 'elem')), may hold values from -6 to 6
- day_cost: int32 [16384], P(('face', 'elem')), may hold values from 0 to 3
- heat_rate: float32 [432], replicated, may hold values from -2 to 2
- coupling: float32 [3, 16384], P(None, ('face', 'elem')), may hold values from 0.2 to 0.7
- metric: float32 [16384], P(('face', 'elem')), may hold values from 0.5 to 2
- stencil: float32 [16, 16], replicated, may hold values from -1.5 to 1.5
- phys_owner: int32 [8192, 1], P(('face', 'elem')), may hold values from 0 to 7; in each aligned block of 256 rows (0 to 255, 256 to 511, ...) at most 64 rows name the same one
- edge_table: int32 [1024, 4], P(('face', 'elem')), may hold values from 0 to 63
- kept_inverse: float32 [1296, 8192], P(None, ('face', 'elem')), may hold values from -0.6 to 1.3
- slot_inverse: float32 [1296, 16384], P(None, ('face', 'elem')), may hold values from -0.6 to 1.3
Outputs:
- new_state: float32 [432, 16384], P(None, ('face', 'elem'))
Inputs may be any that keep to these rules, and one draw needn't show every extreme that they name: `phys_owner`: in each aligned block of 256 entries (the sent columns of one device) no value appears more than 64 times, and some value appears exactly 64 times.
All inputs are finite; a program needn't handle non-finite values.
Results may differ from a plain program's by a relative error of at most 0.0003.
Values sent between devices are 32-bit elements; how exact they have to be, the bound alone decides.
A program may use at most 64 MiB of HBM per device.

v0:
```python
import functools

import jax
import jax.numpy as jnp
import numpy as np
from jax import lax
from jax.experimental import pallas as pl
from jax.experimental.pallas import tpu as pltpu
from jax.sharding import PartitionSpec as P

FIELDS = 6
LEV = 72
BLK = 18
NB = 4
NP = 4
PTS = NP * NP
SWEEPS = 3
RIM_E = 16
VISC_COEF = 0.2
LANES = 128
ROWS = FIELDS * LEV
HALF_ROWS = ROWS // 2
PAIRS = BLK * BLK
REC = HALF_ROWS + 8
MESH = pl.DeviceIdType.MESH
HIGHEST = lax.Precision.HIGHEST
F32 = jnp.float32
BF16 = jnp.bfloat16


def iota(shape, dim):
    return lax.broadcasted_iota(jnp.int32, shape, dim)


def split(x):
    hi = x.astype(BF16)
    lo = (x - hi.astype(F32)).astype(BF16)
    return hi, lo


def exact_dot(x, picks, dims=((1,), (0,))):
    hi, lo = split(x)
    total = lax.dot_general(hi, picks, (dims, ((), ())), preferred_element_type=F32)
    return total + lax.dot_general(lo, picks, (dims, ((), ())), preferred_element_type=F32)


def kernel(
    groups,
    field_ref, day_ref, heat_ref, couple_ref, metric_ref, stencil_ref, owner_ref, edge_ref,
    kept_hbm, slot_hbm,
    out_ref,
    kept_raw, slot_raw, slot_inv, kept_src, kept_val, send_buf, recv_buf, slot_val, slot_y0,
    ret_buf, home_buf, upd, lap1, lap2, low1, high1, low2, high2, picks, route,
    load_sem, s1_sem, r1_sem, s2_sem, r2_sem, hs_sem, hr_sem,
):
    face = lax.axis_index("face")
    me = lax.axis_index("elem")
    partner = face + 1 - 2 * lax.rem(face, 2)
    right = lax.rem(me + 1, groups)
    left = lax.rem(me + groups - 1, groups)
    cap = 512 // groups
    inv_rows = NB * PAIRS

    loads = []
    for c in range(2):
        loads.append(pltpu.make_async_copy(
            kept_hbm.at[:, pl.ds(c * LANES, LANES)], kept_raw.at[pl.ds(c * inv_rows, inv_rows)],
            load_sem.at[c]))
    for a in range(groups):
        loads.append(pltpu.make_async_copy(
            slot_hbm.at[:, pl.ds((a // 2) * LANES, LANES)],
            slot_raw.at[pl.ds(a * inv_rows, inv_rows)], load_sem.at[2 + a]))
    for one in loads:
        one.start()

    barrier = pltpu.get_barrier_semaphore()
    for o in range(groups):
        pl.semaphore_signal(barrier, inc=1, device_id=(partner, jnp.int32(o)), device_id_type=MESH)
    for o in (left, right):
        pl.semaphore_signal(barrier, inc=1, device_id=(face, o), device_id_type=MESH)

    owner = owner_ref[...]
    named = iota((groups, 256), 0) == owner
    earlier = (iota((256, 256), 0) < iota((256, 256), 1)).astype(BF16)
    before = jnp.dot(named.astype(BF16), earlier, preferred_element_type=F32)
    rank = jnp.sum(jnp.where(named, before, 0.0), axis=0, keepdims=True).astype(jnp.int32)
    spot = owner * LANES + rank
    spot2 = jnp.concatenate([spot, spot + cap], axis=1)
    route[...] = (iota((groups * LANES, 512), 0) == spot2).astype(BF16)

    outer = (((0,), (0,)), ((), ()))
    day = day_ref[...].astype(F32)
    heating = lax.dot_general(heat_ref[...], day, outer, precision=HIGHEST, preferred_element_type=F32)
    source = field_ref[...] + heating
    couple = couple_ref[...]
    sent_couple = couple[:, 256:]
    tail = jnp.concatenate(
        [jnp.concatenate([sent_couple, sent_couple], axis=1), jnp.zeros((5, 512), F32)], axis=0)
    body = jnp.concatenate([source[:HALF_ROWS, 256:], source[HALF_ROWS:, 256:]], axis=1)
    record = exact_dot(jnp.concatenate([body, tail], axis=0), route[...], ((1,), (1,)))
    for o in range(groups):
        send_buf[o] = record[:, o * LANES:(o + 1) * LANES]
    for f in range(FIELDS):
        for c in range(2):
            kept_src[pl.ds((f * 2 + c) * LEV, LEV), :] = source[
                f * LEV:(f + 1) * LEV, c * LANES:(c + 1) * LANES]

    pl.semaphore_wait(barrier, groups + 2)

    def to_owner(o):
        return pltpu.make_async_remote_copy(
            src_ref=send_buf.at[o], dst_ref=recv_buf.at[me], send_sem=s1_sem.at[o],
            recv_sem=r1_sem.at[me], device_id=(partner, o), device_id_type=MESH)

    def from_home(a):
        return pltpu.make_async_remote_copy(
            src_ref=send_buf.at[a], dst_ref=recv_buf.at[a], send_sem=s1_sem.at[a],
            recv_sem=r1_sem.at[a], device_id=(partner, a), device_id_type=MESH)

    for k in range(groups):
        to_owner(lax.rem(me + k, groups)).start()

    for one in loads[:2]:
        one.wait()

    def kept_value(j, _):
        for f in range(FIELDS):
            kept_val[f * BLK + j] = kept_src[pl.ds(f * 2 * LEV + j, 8, stride=BLK), :]
        return 0

    lax.fori_loop(0, BLK, kept_value, 0)

    def kept_m(ij):
        return kept_raw[pl.ds(ij, 8, stride=PAIRS), :]

    def kept_row(i):
        sums = [None] * FIELDS
        for j in range(BLK):
            m = kept_m(i * BLK + j)
            for f in range(FIELDS):
                term = m * kept_val[f * BLK + j]
                sums[f] = term if sums[f] is None else sums[f] + term
        return sums

    first = kept_row(0)
    last = kept_row(BLK - 1)
    ends = (kept_m(0), kept_m(BLK - 1), kept_m((BLK - 1) * BLK), kept_m(PAIRS - 1))
    gap = jnp.zeros((1, LANES), F32)
    pieces_low, pieces_high = [], []
    for c in range(2):
        rows = [couple[k:k + 1, c * LANES:(c + 1) * LANES] for k in range(NB - 1)]
        pieces_low += [gap] + rows
        pieces_high += rows + [gap]
    c_low = jnp.concatenate(pieces_low, axis=0)
    c_high = jnp.concatenate(pieces_high, axis=0)

    def kept_drive(e0, e17):
        return c_low * pltpu.roll(e17, 1, 0), c_high * pltpu.roll(e0, 7, 0)

    drives = []
    for f in range(FIELDS):
        e0, e17 = first[f], last[f]
        for _ in range(SWEEPS - 1):
            lo, hi = kept_drive(e0, e17)
            e0 = first[f] + ends[0] * lo + ends[1] * hi
            e17 = last[f] + ends[2] * lo + ends[3] * hi
        drives.append(kept_drive(e0, e17))
    for f in range(FIELDS):
        slot_y0[2 * f] = drives[f][0]
        slot_y0[2 * f + 1] = drives[f][1]

    def kept_final(i, _):
        sums = kept_row(i)
        m0, m1 = kept_m(i * BLK), kept_m(i * BLK + BLK - 1)
        for f in range(FIELDS):
            y = sums[f] + m0 * slot_y0[2 * f] + m1 * slot_y0[2 * f + 1]
            kept_src[pl.ds(f * 2 * LEV + i, 8, stride=BLK), :] = y
        return 0

    lax.fori_loop(0, BLK, kept_final, 0)
    for c in range(2):
        upd[c] = jnp.concatenate(
            [kept_src[pl.ds((f * 2 + c) * LEV, LEV), :] for f in range(FIELDS)], axis=0)

    spread = (lax.rem(iota((PTS, LANES), 1), PTS) == iota((PTS, LANES), 0)).astype(F32)
    part = jnp.dot(stencil_ref[...], spread, precision=HIGHEST, preferred_element_type=F32)
    full = lax.dot_general(part, spread, outer, precision=HIGHEST, preferred_element_type=F32)
    same = iota((LANES, LANES), 0) // PTS == iota((LANES, LANES), 1) // PTS
    operator = jnp.where(same, full, 0.0)

    def laplace(x, c):
        applied = jnp.dot(x, operator, precision=HIGHEST, preferred_element_type=F32)
        return applied * metric_ref[:, c * LANES:(c + 1) * LANES]

    def to_left(lap, high, n):
        return pltpu.make_async_remote_copy(
            src_ref=lap.at[pl.ds(0, 2)], dst_ref=high, send_sem=hs_sem.at[n], recv_sem=hr_sem.at[n],
            device_id=(face, left), device_id_type=MESH)

    def to_right(lap, low, n):
        return pltpu.make_async_remote_copy(
            src_ref=lap.at[pl.ds(2, 2)], dst_ref=low, send_sem=hs_sem.at[n], recv_sem=hr_sem.at[n],
            device_id=(face, right), device_id_type=MESH)

    for c in range(2):
        lap1[c] = laplace(upd[c], c)
    left1 = to_left(lap1, high1, 0)
    left1.start()

    col = iota((1, 512), 1)
    point = lax.rem(col, PTS)
    pi, pj = point // NP, lax.rem(point, NP)
    place = (iota((32, 512), 1) // PTS == iota((32, 512), 0)).astype(F32)
    table = jnp.dot(edge_ref[...].astype(F32), place, preferred_element_type=F32).astype(jnp.int32) * PTS
    flip_i = (NP - 1 - pi) * NP + pj
    flip_j = pi * NP + NP - 1 - pj
    vert = jnp.where(pi == 0, table[0:1] + flip_i, jnp.where(pi == NP - 1, table[2:3] + flip_i, -1))
    hori = jnp.where(pj == NP - 1, table[1:2] + flip_j, jnp.where(pj == 0, table[3:4] + flip_j, -1))
    for k in range(8):
        row = iota((LANES, 512), 0) + k * LANES
        count = (row == col + 256).astype(F32) + (row == vert).astype(F32) + (row == hori).astype(F32)
        picks[pl.ds(k * LANES, LANES), :] = count.astype(BF16)
    share = 1.0 / (1.0 + jnp.where((pi == 0) | (pi == NP - 1), 1.0, 0.0)
                   + jnp.where((pj == 0) | (pj == NP - 1), 1.0, 0.0))

    for one in loads[2:]:
        one.wait()
    plain = (iota((8, LANES), 1) < cap) == (lax.rem(iota((8, LANES), 0), 2) == 0)

    def slot_pair(step, _):
        for u in range(BLK):
            r = step * BLK + u
            x = slot_raw[pl.ds(r, 8, stride=inv_rows), :]
            slot_inv[r] = jnp.where(plain, x, pltpu.roll(x, cap, 1))
        return 0

    lax.fori_loop(0, NB * BLK, slot_pair, 0)

    for a in range(groups):
        from_home(a).wait_recv()

    recv_flat = recv_buf.reshape(groups * REC, LANES)
    ret_flat = ret_buf.reshape(groups * HALF_ROWS, LANES)

    def slot_value(step, _):
        for u in range(8):
            r = step * 8 + u
            slot_val[r] = recv_flat[pl.ds(r, 8, stride=REC), :]
        return 0

    lax.fori_loop(0, REC // 8, slot_value, 0)
    half_fields = FIELDS // 2

    def slot_row(bi, b):
        sums = [None] * half_fields
        for j in range(BLK):
            m = slot_inv[bi * BLK + j]
            for f in range(half_fields):
                term = m * slot_val[f * LEV + b * BLK + j]
                sums[f] = term if sums[f] is None else sums[f] + term
        return sums

    for b in range(NB):
        def slot_first(i, _):
            sums = slot_row(b * BLK + i, b)
            for f in range(half_fields):
                slot_y0[f * LEV + b * BLK + i] = sums[f]
            return 0

        lax.fori_loop(0, BLK, slot_first, 0)

    between = [slot_val[HALF_ROWS + k] for k in range(NB - 1)]

    def slot_drive(e0, e17):
        lo = [None] + [between[b - 1] * e17[b - 1] for b in range(1, NB)]
        hi = [between[b] * e0[b + 1] for b in range(NB - 1)] + [None]
        return lo, hi

    def driven(y, b, i, lo, hi):
        if lo is not None:
            y = y + slot_inv[(b * BLK + i) * BLK] * lo
        if hi is not None:
            y = y + slot_inv[(b * BLK + i) * BLK + BLK - 1] * hi
        return y

    for f in range(half_fields):
        e0 = [slot_y0[f * LEV + b * BLK] for b in range(NB)]
        e17 = [slot_y0[f * LEV + b * BLK + BLK - 1] for b in range(NB)]
        first, last = e0, e17
        for _ in range(SWEEPS - 1):
            lo, hi = slot_drive(e0, e17)
            e0 = [driven(first[b], b, 0, lo[b], hi[b]) for b in range(NB)]
            e17 = [driven(last[b], b, BLK - 1, lo[b], hi[b]) for b in range(NB)]
        lo, hi = slot_drive(e0, e17)

        def slot_final(i, _):
            for b in range(NB):
                r = f * LEV + b * BLK + i
                ret_flat[pl.ds(r, 8, stride=HALF_ROWS), :] = driven(slot_y0[r], b, i, lo[b], hi[b])
            return 0

        lax.fori_loop(0, BLK, slot_final, 0)

    def to_home(a):
        return pltpu.make_async_remote_copy(
            src_ref=ret_buf.at[a], dst_ref=home_buf.at[me], send_sem=s2_sem.at[a],
            recv_sem=r2_sem.at[me], device_id=(partner, a), device_id_type=MESH)

    def from_owner(o):
        return pltpu.make_async_remote_copy(
            src_ref=ret_buf.at[o], dst_ref=home_buf.at[o], send_sem=s2_sem.at[o],
            recv_sem=r2_sem.at[o], device_id=(partner, o), device_id_type=MESH)

    for k in range(groups):
        to_home(lax.rem(me + k, groups)).start()
    for o in range(groups):
        from_owner(o).wait_recv()
    home = jnp.concatenate([home_buf[o] for o in range(groups)], axis=1)
    back = exact_dot(home, route[...])
    for c in range(2):
        upd[2 + c] = jnp.concatenate(
            [back[:, c * LANES:(c + 1) * LANES], back[:, (2 + c) * LANES:(3 + c) * LANES]], axis=0)
    for c in (2, 3):
        lap1[c] = laplace(upd[c], c)
    right1 = to_right(lap1, low1, 1)
    right1.start()

    def own_sum(lap):
        mine = jnp.concatenate([lap[c] for c in range(4)], axis=1)
        return exact_dot(mine, picks[pl.ds(256, 512), :])

    def rim_sum(rim, start):
        both = jnp.concatenate([rim[0], rim[1]], axis=1)
        return exact_dot(both, picks[pl.ds(start, 256), :])

    total = own_sum(lap1)
    left1.wait_recv()
    total = total + rim_sum(high1, 768)
    right1.wait_recv()
    first_pass = (total + rim_sum(low1, 0)) * share
    left2 = to_left(lap2, high2, 2)
    right2 = to_right(lap2, low2, 3)
    for c in range(2):
        lap2[c] = laplace(first_pass[:, c * LANES:(c + 1) * LANES], c)
    left2.start()
    for c in (2, 3):
        lap2[c] = laplace(first_pass[:, c * LANES:(c + 1) * LANES], c)
    right2.start()
    total = own_sum(lap2)
    left2.wait_recv()
    total = total + rim_sum(high2, 768)
    right2.wait_recv()
    second = (total + rim_sum(low2, 0)) * share
    for c in range(4):
        out_ref[:, c * LANES:(c + 1) * LANES] = (
            upd[c] - VISC_COEF * second[:, c * LANES:(c + 1) * LANES])

    for k in range(groups):
        to_owner(jnp.int32(k)).wait_send()
        to_home(jnp.int32(k)).wait_send()
    for one in (left1, right1, left2, right2):
        one.wait_send()


def fused(field_state, day_cost, heat_rate, coupling, metric, stencil, phys_owner, edge_table,
          kept_inverse, slot_inverse):
    groups = lax.axis_size("elem")
    cols = field_state.shape[1]
    inv_rows = NB * PAIRS
    vmem = pl.BlockSpec(memory_space=pltpu.VMEM)
    anywhere = pl.BlockSpec(memory_space=pl.ANY)
    dma = pltpu.SemaphoreType.DMA
    rim = pltpu.VMEM((2, ROWS, LANES), F32)
    whole = pltpu.VMEM((4, ROWS, LANES), F32)
    return pl.pallas_call(
        functools.partial(kernel, groups),
        out_shape=jax.ShapeDtypeStruct((ROWS, cols), F32),
        in_specs=[vmem] * 8 + [anywhere] * 2,
        out_specs=vmem,
        scratch_shapes=[
            pltpu.VMEM((2 * inv_rows, LANES), F32),
            pltpu.VMEM((groups * inv_rows, LANES), F32),
            pltpu.VMEM((inv_rows, 8, LANES), F32),
            pltpu.VMEM((2 * ROWS, LANES), F32),
            pltpu.VMEM((FIELDS * BLK, 8, LANES), F32),
            pltpu.VMEM((groups, REC, LANES), F32),
            pltpu.VMEM((groups, REC, LANES), F32),
            pltpu.VMEM((REC, 8, LANES), F32),
            pltpu.VMEM((HALF_ROWS, 8, LANES), F32),
            pltpu.VMEM((groups, HALF_ROWS, LANES), F32),
            pltpu.VMEM((groups, HALF_ROWS, LANES), F32),
            whole, whole, whole,
            rim, rim, rim, rim,
            pltpu.VMEM((8 * LANES, 512), BF16),
            pltpu.VMEM((groups * LANES, 512), BF16),
            dma((2 + groups,)), dma((groups,)), dma((groups,)), dma((groups,)), dma((groups,)),
            dma((4,)), dma((4,)),
        ],
        compiler_params=pltpu.CompilerParams(
            collective_id=0, has_side_effects=True, vmem_limit_bytes=48 * 2**20),
    )(
        field_state, day_cost.reshape(1, -1), heat_rate.reshape(1, -1), coupling,
        metric.reshape(1, -1), stencil, phys_owner.reshape(1, -1), edge_table.T,
        kept_inverse, slot_inverse,
    )


def swapped(value):
    pairs = [(source, source ^ 1) for source in range(lax.axis_size("face"))]
    return lax.ppermute(value, "face", pairs)


def block_apply(blocks, values):
    result = jnp.zeros(values.shape, F32)
    for j in range(BLK):
        result = result + blocks[None, :, :, j, :] * values[:, :, j, None, :]
    return result


def physics(source, inverse, couple):
    count_n = source.shape[1]
    values = source.reshape(FIELDS, NB, BLK, count_n)
    blocks = inverse.reshape(NB, BLK, BLK, count_n)
    state = block_apply(blocks, values)
    for _ in range(SWEEPS):
        driven = values.at[:, 1:, 0, :].add(couple[None] * state[:, :-1, BLK - 1, :])
        driven = driven.at[:, :-1, BLK - 1, :].add(couple[None] * state[:, 1:, 0, :])
        state = block_apply(blocks, driven)
    return state.reshape(FIELDS * LEV, count_n)


def general(field_state, day_cost, heat_rate, coupling, metric, stencil, phys_owner, edge_table,
            kept_inverse, slot_inverse):
    cols = field_state.shape[1]
    half = cols // 2
    groups = lax.axis_size("elem")
    cap = cols // groups
    source = field_state + day_cost[None, :].astype(F32) * heat_rate[:, None]
    owners = phys_owner[:, 0]
    named = (owners[:, None] == jnp.arange(groups)[None, :]).astype(F32)
    places = jnp.arange(half)
    earlier = (places[None, :] < places[:, None]).astype(F32)
    rank = jnp.sum(jnp.dot(earlier, named, precision=HIGHEST) * named, axis=1).astype(jnp.int32)
    route = ((owners * cap + rank)[:, None] == jnp.arange(cols)[None, :]).astype(F32)
    record = jnp.concatenate([source[:, half:], coupling[:, half:]], axis=0)
    record = jnp.dot(record, route, precision=HIGHEST)
    crossed = swapped(lax.all_to_all(record, "elem", split_axis=1, concat_axis=1, tiled=True))
    done = physics(crossed[:ROWS], slot_inverse, crossed[ROWS:])
    home = lax.all_to_all(swapped(done), "elem", split_axis=1, concat_axis=1, tiled=True)
    sent = jnp.dot(home, route.T, precision=HIGHEST)
    kept = physics(source[:, :half], kept_inverse, coupling[:, :half])
    updated = jnp.concatenate([kept, sent], axis=1)
    rim = RIM_E * PTS
    point = np.arange(cols) % PTS
    pi, pj = point // NP, point % NP
    flip_i, flip_j = (NP - 1 - pi) * NP + pj, pi * NP + NP - 1 - pj
    table = jnp.repeat(edge_table, PTS, axis=0) * PTS
    rows = jnp.arange(cols + 2 * rim)[:, None]
    picks = (rows == jnp.arange(cols)[None, :] + rim).astype(F32)
    sides = ((pi == 0, flip_i), (pj == NP - 1, flip_j), (pi == NP - 1, flip_i), (pj == 0, flip_j))
    divisor = np.ones((cols,), np.float32)
    for k, (mask, match) in enumerate(sides):
        divisor = divisor + mask
        picks = picks + ((rows == (table[:, k] + match)[None, :]) & mask[None, :]).astype(F32)
    operator = jnp.kron(jnp.eye(cols // PTS, dtype=F32), stencil.T)
    ring = [(i, (i + 1) % groups) for i in range(groups)]
    back = [(b, a) for a, b in ring]

    def smooth(x):
        lap = jnp.dot(x, operator, precision=HIGHEST) * metric[None, :]
        low = lax.ppermute(lap[:, cols - rim:], "elem", ring)
        high = lax.ppermute(lap[:, :rim], "elem", back)
        extended = jnp.concatenate([low, lap, high], axis=1)
        return jnp.dot(extended, picks, precision=HIGHEST) / divisor.astype(np.float32)[None, :]

    return updated - VISC_COEF * smooth(smooth(updated))


def solution(mesh):
    in_specs = (
        P(None, ("face", "elem")),
        P(("face", "elem")),
        P(),
        P(None, ("face", "elem")),
        P(("face", "elem")),
        P(),
        P(("face", "elem"), None),
        P(("face", "elem"), None),
        P(None, ("face", "elem")),
        P(None, ("face", "elem")),
    )
    out_specs = P(None, ("face", "elem"))
    local = fused if mesh.shape["elem"] == 8 else general
    return jax.shard_map(local, mesh=mesh, in_specs=in_specs, out_specs=out_specs, check_vma=False)
```

profile of v0, /device:TPU:1, one launch (start us, length us, event | category | flops | bytes accessed | tf_op | source)
XLA Modules:
  0.0 80.6 jit_solution(4043541204721375003)
XLA Ops:
  0.0 0.0 copy-start
  0.0 1.7 %copy-done = f32[1296,512]{1,0:T(8,128)S(1)} copy-done((f32[1296,512]{1,0:T(8,128)S(1)}, f32[1296,512]{1,0:T(8,128)}, u32[]{:S(2)}) %copy-start) | copy-done | bytes 2654232
  1.8 0.0 copy-start.1
  1.8 1.3 %copy-done.1 = f32[1296,256]{1,0:T(8,128)S(1)} copy-done((f32[1296,256]{1,0:T(8,128)S(1)}, f32[1296,256]{1,0:T(8,128)}, u32[]{:S(2)}) %copy-start.1) | copy-done | bytes 1327128
  3.1 0.0 copy-start.2
  3.1 1.2 %copy-done.2 = f32[432,512]{1,0:T(8,128)S(1)} copy-done((f32[432,512]{1,0:T(8,128)S(1)}, f32[432,512]{1,0:T(8,128)}, u32[]{:S(2)}) %copy-start.2) | copy-done | bytes 884760
  4.2 0.0 copy-start.3
  4.2 0.7 copy-done.3
  4.9 0.0 copy-start.4
  4.9 0.7 copy-done.4
  5.6 0.0 copy-start.5
  5.6 0.7 copy-done.5
  6.3 0.0 copy-start.6
  6.3 0.7 copy-done.6
  7.0 0.0 copy-start.7
  7.0 0.7 copy-done.7
  7.7 0.0 copy-start.8
  7.7 0.7 copy-done.8
  8.4 0.0 copy-start.9
  8.4 0.7 copy-done.9
  9.0 70.7 %shard_map.100 = f32[432,512]{1,0:T(8,128)S(1)} custom-call(f32[432,512]{1,0:T(8,128)S(1)} %copy-done.2, s32[1,512]{1,0:T(1,128)S(1)} %bitcast.5, f32[1,432]{1,0:T(1,128)S(1)} %bitcast.6, f32[3,512]{1,0:T(4,128)S(1)} %copy-done.3, f32[1,512]{1,0:T(1,128)S(1)} %bitcast.7, f32[16,16]{1,0:T(8,128)S(1)} %copy-done.4, s32[1,256]{1,0:T(1,128)S(1)} %bitcast.9, ...), custom_call_target="tpu_custom_call" | custom-call | tf_op jit(solution)/shard_map/pallas_call | solution.py:375
  79.7 0.9 %copy.12 = f32[432,512]{1,0:T(8,128)} copy(f32[432,512]{1,0:T(8,128)S(1)} %shard_map.100) | data formatting | bytes 1769472
Async XLA Ops:
  0.0 1.7 %copy-start = (f32[1296,512]{1,0:T(8,128)S(1)}, f32[1296,512]{1,0:T(8,128)}, u32[]{:S(2)}) copy-start(f32[1296,512]{1,0:T(8,128)} %slot_hbm.1) | copy-start | bytes 7962628
  1.8 1.3 %copy-start.1 = (f32[1296,256]{1,0:T(8,128)S(1)}, f32[1296,256]{1,0:T(8,128)}, u32[]{:S(2)}) copy-start(f32[1296,256]{1,0:T(8,128)} %kept_hbm.1) | copy-start | bytes 3981316
  3.1 1.2 %copy-start.2 = (f32[432,512]{1,0:T(8,128)S(1)}, f32[432,512]{1,0:T(8,128)}, u32[]{:S(2)}) copy-start(f32[432,512]{1,0:T(8,128)} %field_ref.1) | copy-start | bytes 2654212
  4.2 0.7 copy-start.3
  4.9 0.7 copy-start.4
  5.6 0.7 copy-start.5
  6.3 0.7 copy-start.6
  7.0 0.7 copy-start.7
  7.7 0.7 copy-start.8
  8.4 0.7 copy-start.9
where the time goes:
time: 81 us; the launch traced here: 80.6 us
  Pallas kernels  70.7 us (87%)
  local copies, waits for them, and re-layouts  9.95 us (12%)
    pallas_call x1, Pallas kernels, fused(): pl.pallas_call(functools.partial(kernel, groups), out_shape=jax.ShapeDtyp...  70.7 us
    unnamed x21, local copies, waits for them, and re-layouts  9.95 us

commit v1 on v0

--- a/solution.py
+++ b/solution.py
@@ -19,9 +19,8 @@
 VISC_COEF = 0.2
 LANES = 128
 ROWS = FIELDS * LEV
-HALF_ROWS = ROWS // 2
 PAIRS = BLK * BLK
-REC = HALF_ROWS + 8
+PIECES = FIELDS // 2
 MESH = pl.DeviceIdType.MESH
 HIGHEST = lax.Precision.HIGHEST
 F32 = jnp.float32
@@ -40,8 +39,9 @@
 
 def exact_dot(x, picks, dims=((1,), (0,))):
     hi, lo = split(x)
-    total = lax.dot_general(hi, picks, (dims, ((), ())), preferred_element_type=F32)
-    return total + lax.dot_general(lo, picks, (dims, ((), ())), preferred_element_type=F32)
+    both = jnp.concatenate([hi, lo], axis=0)
+    total = lax.dot_general(both, picks, (dims, ((), ())), preferred_element_type=F32)
+    return total[:x.shape[0]] + total[x.shape[0]:]
 
 
 def kernel(
@@ -49,8 +49,9 @@
     field_ref, day_ref, heat_ref, couple_ref, metric_ref, stencil_ref, owner_ref, edge_ref,
     kept_hbm, slot_hbm,
     out_ref,
-    kept_raw, slot_raw, slot_inv, kept_src, kept_val, send_buf, recv_buf, slot_val, slot_y0,
-    ret_buf, home_buf, upd, lap1, lap2, low1, high1, low2, high2, picks, route,
+    kept_raw, slot_raw, slot_inv, kept_src, kept_val, drive,
+    send0, send1, send2, recv0, recv1, recv2, slot_val, slot_y0,
+    ret0, ret1, ret2, home_buf, upd, lap1, lap2, low1, high1, low2, high2, picks, route,
     load_sem, s1_sem, r1_sem, s2_sem, r2_sem, hs_sem, hr_sem,
 ):
     face = lax.axis_index("face")
@@ -60,6 +61,7 @@
     left = lax.rem(me + groups - 1, groups)
     cap = 512 // groups
     inv_rows = NB * PAIRS
+    sends, recvs, rets = (send0, send1, send2), (recv0, recv1, recv2), (ret0, ret1, ret2)
 
     loads = []
     for c in range(2):
@@ -79,6 +81,26 @@
     for o in (left, right):
         pl.semaphore_signal(barrier, inc=1, device_id=(face, o), device_id_type=MESH)
 
+    def to_owner(o, p):
+        return pltpu.make_async_remote_copy(
+            src_ref=sends[p].at[o], dst_ref=recvs[p].at[me], send_sem=s1_sem.at[p, o],
+            recv_sem=r1_sem.at[p, me], device_id=(partner, o), device_id_type=MESH)
+
+    def from_home(a, p):
+        return pltpu.make_async_remote_copy(
+            src_ref=sends[p].at[a], dst_ref=recvs[p].at[a], send_sem=s1_sem.at[p, a],
+            recv_sem=r1_sem.at[p, a], device_id=(partner, a), device_id_type=MESH)
+
+    def to_home(a, p):
+        return pltpu.make_async_remote_copy(
+            src_ref=rets[p].at[a], dst_ref=home_buf.at[p, me], send_sem=s2_sem.at[p, a],
+            recv_sem=r2_sem.at[p, me], device_id=(partner, a), device_id_type=MESH)
+
+    def from_owner(o, p):
+        return pltpu.make_async_remote_copy(
+            src_ref=rets[p].at[o], dst_ref=home_buf.at[p, o], send_sem=s2_sem.at[p, o],
+            recv_sem=r2_sem.at[p, o], device_id=(partner, o), device_id_type=MESH)
+
     owner = owner_ref[...]
     named = iota((groups, 256), 0) == owner
     earlier = (iota((256, 256), 0) < iota((256, 256), 1)).astype(BF16)
@@ -96,29 +118,102 @@
     sent_couple = couple[:, 256:]
     tail = jnp.concatenate(
         [jnp.concatenate([sent_couple, sent_couple], axis=1), jnp.zeros((5, 512), F32)], axis=0)
-    body = jnp.concatenate([source[:HALF_ROWS, 256:], source[HALF_ROWS:, 256:]], axis=1)
-    record = exact_dot(jnp.concatenate([body, tail], axis=0), route[...], ((1,), (1,)))
-    for o in range(groups):
-        send_buf[o] = record[:, o * LANES:(o + 1) * LANES]
+    for p in range(PIECES):
+        body = jnp.concatenate(
+            [source[p * LEV:(p + 1) * LEV, 256:], source[(p + 3) * LEV:(p + 4) * LEV, 256:]], axis=1)
+        if p == 0:
+            body = jnp.concatenate([body, tail], axis=0)
+        record = exact_dot(body, route[...], ((1,), (1,)))
+        for o in range(groups):
+            sends[p][o] = record[:, o * LANES:(o + 1) * LANES]
+        if p == 0:
+            pl.semaphore_wait(barrier, groups + 2)
+        for k in range(groups):
+            to_owner(lax.rem(me + k, groups), p).start()
     for f in range(FIELDS):
         for c in range(2):
             kept_src[pl.ds((f * 2 + c) * LEV, LEV), :] = source[
                 f * LEV:(f + 1) * LEV, c * LANES:(c + 1) * LANES]
 
-    pl.semaphore_wait(barrier, groups + 2)
-
-    def to_owner(o):
-        return pltpu.make_async_remote_copy(
-            src_ref=send_buf.at[o], dst_ref=recv_buf.at[me], send_sem=s1_sem.at[o],
-            recv_sem=r1_sem.at[me], device_id=(partner, o), device_id_type=MESH)
-
-    def from_home(a):
-        return pltpu.make_async_remote_copy(
-            src_ref=send_buf.at[a], dst_ref=recv_buf.at[a], send_sem=s1_sem.at[a],
-            recv_sem=r1_sem.at[a], device_id=(partner, a), device_id_type=MESH)
-
-    for k in range(groups):
-        to_owner(lax.rem(me + k, groups)).start()
+    for one in loads[2:]:
+        one.wait()
+    plain = (iota((8, LANES), 1) < cap) == (lax.rem(iota((8, LANES), 0), 2) == 0)
+
+    def slot_pair(step, _):
+        for u in range(BLK):
+            r = step * BLK + u
+            x = slot_raw[pl.ds(r, 8, stride=inv_rows), :]
+            slot_inv[r] = jnp.where(plain, x, pltpu.roll(x, cap, 1))
+        return 0
+
+    lax.fori_loop(0, NB * BLK, slot_pair, 0)
+
+    slot_m = slot_inv
+
+    def slot_piece(p):
+        for a in range(groups):
+            from_home(a, p).wait_recv()
+        rows = LEV + 8 if p == 0 else LEV
+        recv_flat = recvs[p].reshape(groups * rows, LANES)
+        ret_flat = rets[p].reshape(groups * LEV, LANES)
+
+        def slot_value(step, _):
+            for u in range(8):
+                slot_val[step * 8 + u] = recv_flat[pl.ds(step * 8 + u, 8, stride=rows), :]
+            return 0
+
+        lax.fori_loop(0, LEV // 8, slot_value, 0)
+        if p == 0:
+            for k in range(NB - 1):
+                slot_val[LEV + k] = recv_flat[pl.ds(LEV + k, 8, stride=rows), :]
+
+        for b in range(NB):
+            values = [slot_val[b * BLK + j] for j in range(BLK)]
+
+            def slot_first(i, _):
+                sums = [slot_m[(b * BLK + i) * BLK + j] * values[j] for j in range(BLK)]
+                while len(sums) > 1:
+                    pairs = [sums[k] + sums[k + 1] for k in range(0, len(sums) - 1, 2)]
+                    sums = pairs + sums[len(pairs) * 2:]
+                slot_y0[b * BLK + i] = sums[0]
+                return 0
+
+            lax.fori_loop(0, BLK, slot_first, 0)
+
+        between = [slot_val[LEV + k] for k in range(NB - 1)]
+
+        def slot_drive(e0, e17):
+            lo = [None] + [between[b - 1] * e17[b - 1] for b in range(1, NB)]
+            hi = [between[b] * e0[b + 1] for b in range(NB - 1)] + [None]
+            return lo, hi
+
+        def driven(y, b, i, lo, hi):
+            if lo is not None:
+                y = y + slot_m[(b * BLK + i) * BLK] * lo
+            if hi is not None:
+                y = y + slot_m[(b * BLK + i) * BLK + BLK - 1] * hi
+            return y
+
+        e0 = first = [slot_y0[b * BLK] for b in range(NB)]
+        e17 = last = [slot_y0[b * BLK + BLK - 1] for b in range(NB)]
+        for _ in range(SWEEPS - 1):
+            lo, hi = slot_drive(e0, e17)
+            e0 = [driven(first[b], b, 0, lo[b], hi[b]) for b in range(NB)]
+            e17 = [driven(last[b], b, BLK - 1, lo[b], hi[b]) for b in range(NB)]
+        lo, hi = slot_drive(e0, e17)
+
+        def slot_final(i, _):
+            for b in range(NB):
+                r = b * BLK + i
+                ret_flat[pl.ds(r, 8, stride=LEV), :] = driven(slot_y0[r], b, i, lo[b], hi[b])
+            return 0
+
+        lax.fori_loop(0, BLK, slot_final, 0)
+        for k in range(groups):
+            to_home(lax.rem(me + k, groups), p).start()
+
+    for p in range(PIECES):
+        slot_piece(p)
 
     for one in loads[:2]:
         one.wait()
@@ -166,21 +261,22 @@
             e17 = last[f] + ends[2] * lo + ends[3] * hi
         drives.append(kept_drive(e0, e17))
     for f in range(FIELDS):
-        slot_y0[2 * f] = drives[f][0]
-        slot_y0[2 * f + 1] = drives[f][1]
+        drive[2 * f] = drives[f][0]
+        drive[2 * f + 1] = drives[f][1]
 
     def kept_final(i, _):
         sums = kept_row(i)
         m0, m1 = kept_m(i * BLK), kept_m(i * BLK + BLK - 1)
         for f in range(FIELDS):
-            y = sums[f] + m0 * slot_y0[2 * f] + m1 * slot_y0[2 * f + 1]
+            y = sums[f] + m0 * drive[2 * f] + m1 * drive[2 * f + 1]
             kept_src[pl.ds(f * 2 * LEV + i, 8, stride=BLK), :] = y
         return 0
 
     lax.fori_loop(0, BLK, kept_final, 0)
-    for c in range(2):
-        upd[c] = jnp.concatenate(
-            [kept_src[pl.ds((f * 2 + c) * LEV, LEV), :] for f in range(FIELDS)], axis=0)
+    for p in range(PIECES):
+        for c in range(2):
+            upd[p, c] = jnp.concatenate(
+                [kept_src[pl.ds((f * 2 + c) * LEV, LEV), :] for f in (p, p + 3)], axis=0)
 
     spread = (lax.rem(iota((PTS, LANES), 1), PTS) == iota((PTS, LANES), 0)).astype(F32)
     part = jnp.dot(stencil_ref[...], spread, precision=HIGHEST, preferred_element_type=F32)
@@ -192,20 +288,20 @@
         applied = jnp.dot(x, operator, precision=HIGHEST, preferred_element_type=F32)
         return applied * metric_ref[:, c * LANES:(c + 1) * LANES]
 
-    def to_left(lap, high, n):
+    def to_left(lap, high, n, p):
         return pltpu.make_async_remote_copy(
-            src_ref=lap.at[pl.ds(0, 2)], dst_ref=high, send_sem=hs_sem.at[n], recv_sem=hr_sem.at[n],
-            device_id=(face, left), device_id_type=MESH)
-
-    def to_right(lap, low, n):
+            src_ref=lap.at[p, pl.ds(0, 2)], dst_ref=high.at[p], send_sem=hs_sem.at[n, p],
+            recv_sem=hr_sem.at[n, p], device_id=(face, left), device_id_type=MESH)
+
+    def to_right(lap, low, n, p):
         return pltpu.make_async_remote_copy(
-            src_ref=lap.at[pl.ds(2, 2)], dst_ref=low, send_sem=hs_sem.at[n], recv_sem=hr_sem.at[n],
-            device_id=(face, right), device_id_type=MESH)
-
-    for c in range(2):
-        lap1[c] = laplace(upd[c], c)
-    left1 = to_left(lap1, high1, 0)
-    left1.start()
+            src_ref=lap.at[p, pl.ds(2, 2)], dst_ref=low.at[p], send_sem=hs_sem.at[n, p],
+            recv_sem=hr_sem.at[n, p], device_id=(face, right), device_id_type=MESH)
+
+    for p in range(PIECES):
+        for c in range(2):
+            lap1[p, c] = laplace(upd[p, c], c)
+        to_left(lap1, high1, 0, p).start()
 
     col = iota((1, 512), 1)
     point = lax.rem(col, PTS)
@@ -223,143 +319,65 @@
     share = 1.0 / (1.0 + jnp.where((pi == 0) | (pi == NP - 1), 1.0, 0.0)
                    + jnp.where((pj == 0) | (pj == NP - 1), 1.0, 0.0))
 
-    for one in loads[2:]:
-        one.wait()
-    plain = (iota((8, LANES), 1) < cap) == (lax.rem(iota((8, LANES), 0), 2) == 0)
-
-    def slot_pair(step, _):
-        for u in range(BLK):
-            r = step * BLK + u
-            x = slot_raw[pl.ds(r, 8, stride=inv_rows), :]
-            slot_inv[r] = jnp.where(plain, x, pltpu.roll(x, cap, 1))
-        return 0
-
-    lax.fori_loop(0, NB * BLK, slot_pair, 0)
-
-    for a in range(groups):
-        from_home(a).wait_recv()
-
-    recv_flat = recv_buf.reshape(groups * REC, LANES)
-    ret_flat = ret_buf.reshape(groups * HALF_ROWS, LANES)
-
-    def slot_value(step, _):
-        for u in range(8):
-            r = step * 8 + u
-            slot_val[r] = recv_flat[pl.ds(r, 8, stride=REC), :]
-        return 0
-
-    lax.fori_loop(0, REC // 8, slot_value, 0)
-    half_fields = FIELDS // 2
-
-    def slot_row(bi, b):
-        sums = [None] * half_fields
-        for j in range(BLK):
-            m = slot_inv[bi * BLK + j]
-            for f in range(half_fields):
-                term = m * slot_val[f * LEV + b * BLK + j]
-                sums[f] = term if sums[f] is None else sums[f] + term
-        return sums
-
-    for b in range(NB):
-        def slot_first(i, _):
-            sums = slot_row(b * BLK + i, b)
-            for f in range(half_fields):
-                slot_y0[f * LEV + b * BLK + i] = sums[f]
-            return 0
-
-        lax.fori_loop(0, BLK, slot_first, 0)
-
-    between = [slot_val[HALF_ROWS + k] for k in range(NB - 1)]
-
-    def slot_drive(e0, e17):
-        lo = [None] + [between[b - 1] * e17[b - 1] for b in range(1, NB)]
-        hi = [between[b] * e0[b + 1] for b in range(NB - 1)] + [None]
-        return lo, hi
-
-    def driven(y, b, i, lo, hi):
-        if lo is not None:
-            y = y + slot_inv[(b * BLK + i) * BLK] * lo
-        if hi is not None:
-            y = y + slot_inv[(b * BLK + i) * BLK + BLK - 1] * hi
-        return y
-
-    for f in range(half_fields):
-        e0 = [slot_y0[f * LEV + b * BLK] for b in range(NB)]
-        e17 = [slot_y0[f * LEV + b * BLK + BLK - 1] for b in range(NB)]
-        first, last = e0, e17
-        for _ in range(SWEEPS - 1):
-            lo, hi = slot_drive(e0, e17)
-            e0 = [driven(first[b], b, 0, lo[b], hi[b]) for b in range(NB)]
-            e17 = [driven(last[b], b, BLK - 1, lo[b], hi[b]) for b in range(NB)]
-        lo, hi = slot_drive(e0, e17)
-
-        def slot_final(i, _):
-            for b in range(NB):
-                r = f * LEV + b * BLK + i
-                ret_flat[pl.ds(r, 8, stride=HALF_ROWS), :] = driven(slot_y0[r], b, i, lo[b], hi[b])
-            return 0
-
-        lax.fori_loop(0, BLK, slot_final, 0)
-
-    def to_home(a):
-        return pltpu.make_async_remote_copy(
-            src_ref=ret_buf.at[a], dst_ref=home_buf.at[me], send_sem=s2_sem.at[a],
-            recv_sem=r2_sem.at[me], device_id=(partner, a), device_id_type=MESH)
-
-    def from_owner(o):
-        return pltpu.make_async_remote_copy(
-            src_ref=ret_buf.at[o], dst_ref=home_buf.at[o], send_sem=s2_sem.at[o],
-            recv_sem=r2_sem.at[o], device_id=(partner, o), device_id_type=MESH)
-
-    for k in range(groups):
-        to_home(lax.rem(me + k, groups)).start()
-    for o in range(groups):
-        from_owner(o).wait_recv()
-    home = jnp.concatenate([home_buf[o] for o in range(groups)], axis=1)
-    back = exact_dot(home, route[...])
-    for c in range(2):
-        upd[2 + c] = jnp.concatenate(
-            [back[:, c * LANES:(c + 1) * LANES], back[:, (2 + c) * LANES:(3 + c) * LANES]], axis=0)
-    for c in (2, 3):
-        lap1[c] = laplace(upd[c], c)
-    right1 = to_right(lap1, low1, 1)
-    right1.start()
-
-    def own_sum(lap):
-        mine = jnp.concatenate([lap[c] for c in range(4)], axis=1)
+    def own_sum(lap, p):
+        mine = jnp.concatenate([lap[p, c] for c in range(4)], axis=1)
         return exact_dot(mine, picks[pl.ds(256, 512), :])
 
-    def rim_sum(rim, start):
-        both = jnp.concatenate([rim[0], rim[1]], axis=1)
+    def rim_sum(rim, p, start):
+        both = jnp.concatenate([rim[p, 0], rim[p, 1]], axis=1)
         return exact_dot(both, picks[pl.ds(start, 256), :])
 
-    total = own_sum(lap1)
-    left1.wait_recv()
-    total = total + rim_sum(high1, 768)
-    right1.wait_recv()
-    first_pass = (total + rim_sum(low1, 0)) * share
-    left2 = to_left(lap2, high2, 2)
-    right2 = to_right(lap2, low2, 3)
-    for c in range(2):
-        lap2[c] = laplace(first_pass[:, c * LANES:(c + 1) * LANES], c)
-    left2.start()
-    for c in (2, 3):
-        lap2[c] = laplace(first_pass[:, c * LANES:(c + 1) * LANES], c)
-    right2.start()
-    total = own_sum(lap2)
-    left2.wait_recv()
-    total = total + rim_sum(high2, 768)
-    right2.wait_recv()
-    second = (total + rim_sum(low2, 0)) * share
-    for c in range(4):
-        out_ref[:, c * LANES:(c + 1) * LANES] = (
-            upd[c] - VISC_COEF * second[:, c * LANES:(c + 1) * LANES])
-
-    for k in range(groups):
-        to_owner(jnp.int32(k)).wait_send()
-        to_home(jnp.int32(k)).wait_send()
-    for one in (left1, right1, left2, right2):
-        one.wait_send()
+    def at_home(p):
+        for o in range(groups):
+            from_owner(o, p).wait_recv()
+        home = jnp.concatenate([home_buf[p, o] for o in range(groups)], axis=1)
+        back = exact_dot(home, route[...])
+        for c in range(2):
+            upd[p, 2 + c] = jnp.concatenate(
+                [back[:, c * LANES:(c + 1) * LANES], back[:, (2 + c) * LANES:(3 + c) * LANES]], axis=0)
+        for c in (2, 3):
+            lap1[p, c] = laplace(upd[p, c], c)
+        to_right(lap1, low1, 1, p).start()
+
+    def averaged(lap, high, low, n, p):
+        total = own_sum(lap, p)
+        to_left(lap, high, n, p).wait_recv()
+        total = total + rim_sum(high, p, 768)
+        to_right(lap, low, n + 1, p).wait_recv()
+        return (total + rim_sum(low, p, 0)) * share
+
+    def first_round(p):
+        first_pass = averaged(lap1, high1, low1, 0, p)
+        for c in range(4):
+            lap2[p, c] = laplace(first_pass[:, c * LANES:(c + 1) * LANES], c)
+        to_left(lap2, high2, 2, p).start()
+        to_right(lap2, low2, 3, p).start()
+
+    def second_round(p):
+        second = averaged(lap2, high2, low2, 2, p)
+        for c in range(4):
+            lanes = slice(c * LANES, (c + 1) * LANES)
+            new = upd[p, c] - VISC_COEF * second[:, lanes]
+            out_ref[p * LEV:(p + 1) * LEV, lanes] = new[:LEV]
+            out_ref[(p + 3) * LEV:(p + 4) * LEV, lanes] = new[LEV:]
+
+    at_home(0)
+    at_home(1)
+    first_round(0)
+    at_home(2)
+    first_round(1)
+    second_round(0)
+    first_round(2)
+    second_round(1)
+    second_round(2)
+
+    for p in range(PIECES):
+        for k in range(groups):
+            to_owner(jnp.int32(k), p).wait_send()
+            to_home(jnp.int32(k), p).wait_send()
+        for lap, low, high, n in ((lap1, low1, high1, 0), (lap2, low2, high2, 2)):
+            to_left(lap, high, n, p).wait_send()
+            to_right(lap, low, n + 1, p).wait_send()
 
 
 def fused(field_state, day_cost, heat_rate, coupling, metric, stencil, phys_owner, edge_table,
@@ -370,8 +388,10 @@
     vmem = pl.BlockSpec(memory_space=pltpu.VMEM)
     anywhere = pl.BlockSpec(memory_space=pl.ANY)
     dma = pltpu.SemaphoreType.DMA
-    rim = pltpu.VMEM((2, ROWS, LANES), F32)
-    whole = pltpu.VMEM((4, ROWS, LANES), F32)
+    rim = pltpu.VMEM((PIECES, 2, 2 * LEV, LANES), F32)
+    whole = pltpu.VMEM((PIECES, 4, 2 * LEV, LANES), F32)
+    part = pltpu.VMEM((groups, LEV, LANES), F32)
+    part0 = pltpu.VMEM((groups, LEV + 8, LANES), F32)
     return pl.pallas_call(
         functools.partial(kernel, groups),
         out_shape=jax.ShapeDtypeStruct((ROWS, cols), F32),
@@ -383,21 +403,21 @@
             pltpu.VMEM((inv_rows, 8, LANES), F32),
             pltpu.VMEM((2 * ROWS, LANES), F32),
             pltpu.VMEM((FIELDS * BLK, 8, LANES), F32),
-            pltpu.VMEM((groups, REC, LANES), F32),
-            pltpu.VMEM((groups, REC, LANES), F32),
-            pltpu.VMEM((REC, 8, LANES), F32),
-            pltpu.VMEM((HALF_ROWS, 8, LANES), F32),
-            pltpu.VMEM((groups, HALF_ROWS, LANES), F32),
-            pltpu.VMEM((groups, HALF_ROWS, LANES), F32),
+            pltpu.VMEM((2 * FIELDS, 8, LANES), F32),
+            part0, part, part, part0, part, part,
+            pltpu.VMEM((LEV + 8, 8, LANES), F32),
+            pltpu.VMEM((LEV, 8, LANES), F32),
+            part, part, part,
+            pltpu.VMEM((PIECES, groups, LEV, LANES), F32),
             whole, whole, whole,
             rim, rim, rim, rim,
             pltpu.VMEM((8 * LANES, 512), BF16),
             pltpu.VMEM((groups * LANES, 512), BF16),
-            dma((2 + groups,)), dma((groups,)), dma((groups,)), dma((groups,)), dma((groups,)),
-            dma((4,)), dma((4,)),
+            dma((2 + groups,)), dma((PIECES, groups)), dma((PIECES, groups)),
+            dma((PIECES, groups)), dma((PIECES, groups)), dma((4, PIECES)), dma((4, PIECES)),
         ],
         compiler_params=pltpu.CompilerParams(
-            collective_id=0, has_side_effects=True, vmem_limit_bytes=48 * 2**20),
+            collective_id=0, has_side_effects=True, vmem_limit_bytes=60 * 2**20),
     )(
         field_state, day_cost.reshape(1, -1), heat_rate.reshape(1, -1), coupling,
         metric.reshape(1, -1), stencil, phys_owner.reshape(1, -1), edge_table.T,

time: 81 us -> 71.4 us (0.88)
  the two profiles are of different devices: /device:TPU:1 before, /device:TPU:13 now
where the time goes in v1:
time: 71.4 us; the launch traced here: 70.7 us
  Pallas kernels  68.5 us (96%)
  local copies, waits for them, and re-layouts  2.14 us (3%)
    pallas_call x1, Pallas kernels, fused(): pl.pallas_call(functools.partial(kernel, groups), out_shape=jax.ShapeDtyp...  68.5 us
    unnamed x1, local copies, waits for them, and re-layouts  2.14 us

profile of v1, /device:TPU:13, one launch (start us, length us, event | category | flops | bytes accessed | tf_op | source)
XLA Modules:
  0.0 70.7 jit_solution(8908458405930321623)
XLA Ops:
  0.0 68.5 %shard_map.100 = f32[432,512]{1,0:T(8,128)} custom-call(f32[432,512]{1,0:T(8,128)} %field_ref.1, s32[1,512]{1,0:T(1,128)} %bitcast.5, f32[1,432]{1,0:T(1,128)} %bitcast.6, f32[3,512]{1,0:T(4,128)} %couple_ref.1, f32[1,512]{1,0:T(1,128)} %bitcast.7, f32[16,16]{1,0:T(8,128)} %stencil_ref.1, s32[1,256]{1,0:T(1,128)} %bitcast.9, s32[4,32]{1,0:T(4,128)} %bitcast.8, ...), custom_call_target="tpu_custom_call" | custom-call | tf_op jit(solution)/shard_map/pallas_call | solution.py:395
  68.6 2.1 %copy.12 = f32[432,512]{1,0:T(8,128)} copy(f32[432,512]{1,0:T(8,128)} %shard_map.100) | data formatting | bytes 1769472

commit v2 on v1

--- a/solution.py
+++ b/solution.py
@@ -18,6 +18,8 @@
 RIM_E = 16
 VISC_COEF = 0.2
 LANES = 128
+EDGE_PTS = 12
+RIM = RIM_E * EDGE_PTS
 ROWS = FIELDS * LEV
 PAIRS = BLK * BLK
 PIECES = FIELDS // 2
@@ -37,6 +39,13 @@
     return hi, lo
 
 
+def packed(place):
+    p = lax.rem(place, PTS)
+    rank = jnp.where(p == 7, 5, jnp.where(p == 8, 6, jnp.where(p == 11, 7, jnp.where(p > 11, p - 4, p))))
+    inside = (p == 5) | (p == 6) | (p == 9) | (p == 10)
+    return jnp.where(inside, -4096, place // PTS * EDGE_PTS + rank)
+
+
 def exact_dot(x, picks, dims=((1,), (0,))):
     hi, lo = split(x)
     both = jnp.concatenate([hi, lo], axis=0)
@@ -51,7 +60,7 @@
     out_ref,
     kept_raw, slot_raw, slot_inv, kept_src, kept_val, drive,
     send0, send1, send2, recv0, recv1, recv2, slot_val, slot_y0,
-    ret0, ret1, ret2, home_buf, upd, lap1, lap2, low1, high1, low2, high2, picks, route,
+    ret0, ret1, ret2, home_buf, upd, lap1, lap2, low1, high1, low2, high2, out1, out2, picks, rims, pack, route,
     load_sem, s1_sem, r1_sem, s2_sem, r2_sem, hs_sem, hr_sem,
 ):
     face = lax.axis_index("face")
@@ -288,20 +297,32 @@
         applied = jnp.dot(x, operator, precision=HIGHEST, preferred_element_type=F32)
         return applied * metric_ref[:, c * LANES:(c + 1) * LANES]
 
-    def to_left(lap, high, n, p):
+    def to_left(out, high, n, p):
         return pltpu.make_async_remote_copy(
-            src_ref=lap.at[p, pl.ds(0, 2)], dst_ref=high.at[p], send_sem=hs_sem.at[n, p],
+            src_ref=out.at[0, p], dst_ref=high.at[p], send_sem=hs_sem.at[n, p],
             recv_sem=hr_sem.at[n, p], device_id=(face, left), device_id_type=MESH)
 
-    def to_right(lap, low, n, p):
+    def to_right(out, low, n, p):
         return pltpu.make_async_remote_copy(
-            src_ref=lap.at[p, pl.ds(2, 2)], dst_ref=low.at[p], send_sem=hs_sem.at[n, p],
+            src_ref=out.at[1, p], dst_ref=low.at[p], send_sem=hs_sem.at[n, p],
             recv_sem=hr_sem.at[n, p], device_id=(face, right), device_id_type=MESH)
+
+    place512 = iota((512, 2 * RIM), 0)
+    place_now = lax.rem(place512, 256)
+    shift = place512 // 256 * RIM
+    pack[...] = (packed(place_now) + shift == iota((512, 2 * RIM), 1)).astype(BF16)
+
+    def edges(lap, out, side, p):
+        halves = [lap[p, 2 * side + c][h * LEV:(h + 1) * LEV] for h in range(2) for c in range(2)]
+        mine = exact_dot(jnp.concatenate(halves, axis=1), pack[...])
+        for k in range(3):
+            out[side, p, k] = mine[:, k * LANES:(k + 1) * LANES]
 
     for p in range(PIECES):
         for c in range(2):
             lap1[p, c] = laplace(upd[p, c], c)
-        to_left(lap1, high1, 0, p).start()
+        edges(lap1, out1, 0, p)
+        to_left(out1, high1, 0, p).start()
 
     col = iota((1, 512), 1)
     point = lax.rem(col, PTS)
@@ -312,20 +333,31 @@
     flip_j = pi * NP + NP - 1 - pj
     vert = jnp.where(pi == 0, table[0:1] + flip_i, jnp.where(pi == NP - 1, table[2:3] + flip_i, -1))
     hori = jnp.where(pj == NP - 1, table[1:2] + flip_j, jnp.where(pj == 0, table[3:4] + flip_j, -1))
-    for k in range(8):
+    for k in range(4):
         row = iota((LANES, 512), 0) + k * LANES
-        count = (row == col + 256).astype(F32) + (row == vert).astype(F32) + (row == hori).astype(F32)
+        count = ((row == col).astype(F32) + (row + 256 == vert).astype(F32)
+                 + (row + 256 == hori).astype(F32))
         picks[pl.ds(k * LANES, LANES), :] = count.astype(BF16)
+    for side, base in ((0, 0), (1, 768)):
+        found = []
+        for t in (vert, hori):
+            near = (t >= base) & (t < base + 256)
+            found.append(jnp.where(near, packed(jnp.where(near, t - base, 0)), -4096))
+        for h in range(2):
+            row = iota((256, 512), 0) - h * (256 - RIM)
+            count = (row == found[0]).astype(F32) + (row == found[1]).astype(F32)
+            rims[side, h] = count.astype(BF16)
     share = 1.0 / (1.0 + jnp.where((pi == 0) | (pi == NP - 1), 1.0, 0.0)
                    + jnp.where((pj == 0) | (pj == NP - 1), 1.0, 0.0))
 
     def own_sum(lap, p):
         mine = jnp.concatenate([lap[p, c] for c in range(4)], axis=1)
-        return exact_dot(mine, picks[pl.ds(256, 512), :])
-
-    def rim_sum(rim, p, start):
-        both = jnp.concatenate([rim[p, 0], rim[p, 1]], axis=1)
-        return exact_dot(both, picks[pl.ds(start, 256), :])
+        return exact_dot(mine, picks[...])
+
+    def rim_sum(rim, p, side):
+        return jnp.concatenate([
+            exact_dot(jnp.concatenate([rim[p, h], rim[p, h + 1]], axis=1), rims[side, h])
+            for h in range(2)], axis=0)
 
     def at_home(p):
         for o in range(groups):
@@ -337,24 +369,27 @@
                 [back[:, c * LANES:(c + 1) * LANES], back[:, (2 + c) * LANES:(3 + c) * LANES]], axis=0)
         for c in (2, 3):
             lap1[p, c] = laplace(upd[p, c], c)
-        to_right(lap1, low1, 1, p).start()
-
-    def averaged(lap, high, low, n, p):
+        edges(lap1, out1, 1, p)
+        to_right(out1, low1, 1, p).start()
+
+    def averaged(lap, out, high, low, n, p):
         total = own_sum(lap, p)
-        to_left(lap, high, n, p).wait_recv()
-        total = total + rim_sum(high, p, 768)
-        to_right(lap, low, n + 1, p).wait_recv()
+        to_left(out, high, n, p).wait_recv()
+        total = total + rim_sum(high, p, 1)
+        to_right(out, low, n + 1, p).wait_recv()
         return (total + rim_sum(low, p, 0)) * share
 
     def first_round(p):
-        first_pass = averaged(lap1, high1, low1, 0, p)
+        first_pass = averaged(lap1, out1, high1, low1, 0, p)
         for c in range(4):
             lap2[p, c] = laplace(first_pass[:, c * LANES:(c + 1) * LANES], c)
-        to_left(lap2, high2, 2, p).start()
-        to_right(lap2, low2, 3, p).start()
+        edges(lap2, out2, 0, p)
+        to_left(out2, high2, 2, p).start()
+        edges(lap2, out2, 1, p)
+        to_right(out2, low2, 3, p).start()
 
     def second_round(p):
-        second = averaged(lap2, high2, low2, 2, p)
+        second = averaged(lap2, out2, high2, low2, 2, p)
         for c in range(4):
             lanes = slice(c * LANES, (c + 1) * LANES)
             new = upd[p, c] - VISC_COEF * second[:, lanes]
@@ -375,9 +410,9 @@
         for k in range(groups):
             to_owner(jnp.int32(k), p).wait_send()
             to_home(jnp.int32(k), p).wait_send()
-        for lap, low, high, n in ((lap1, low1, high1, 0), (lap2, low2, high2, 2)):
-            to_left(lap, high, n, p).wait_send()
-            to_right(lap, low, n + 1, p).wait_send()
+        for out, low, high, n in ((out1, low1, high1, 0), (out2, low2, high2, 2)):
+            to_left(out, high, n, p).wait_send()
+            to_right(out, low, n + 1, p).wait_send()
 
 
 def fused(field_state, day_cost, heat_rate, coupling, metric, stencil, phys_owner, edge_table,
@@ -388,7 +423,8 @@
     vmem = pl.BlockSpec(memory_space=pltpu.VMEM)
     anywhere = pl.BlockSpec(memory_space=pl.ANY)
     dma = pltpu.SemaphoreType.DMA
-    rim = pltpu.VMEM((PIECES, 2, 2 * LEV, LANES), F32)
+    rim = pltpu.VMEM((PIECES, 3, LEV, LANES), F32)
+    outgoing = pltpu.VMEM((2, PIECES, 3, LEV, LANES), F32)
     whole = pltpu.VMEM((PIECES, 4, 2 * LEV, LANES), F32)
     part = pltpu.VMEM((groups, LEV, LANES), F32)
     part0 = pltpu.VMEM((groups, LEV + 8, LANES), F32)
@@ -410,8 +446,10 @@
             part, part, part,
             pltpu.VMEM((PIECES, groups, LEV, LANES), F32),
             whole, whole, whole,
-            rim, rim, rim, rim,
-            pltpu.VMEM((8 * LANES, 512), BF16),
+            rim, rim, rim, rim, outgoing, outgoing,
+            pltpu.VMEM((512, 512), BF16),
+            pltpu.VMEM((2, 2, 256, 512), BF16),
+            pltpu.VMEM((512, 2 * RIM), BF16),
             pltpu.VMEM((groups * LANES, 512), BF16),
             dma((2 + groups,)), dma((PIECES, groups)), dma((PIECES, groups)),
             dma((PIECES, groups)), dma((PIECES, groups)), dma((4, PIECES)), dma((4, PIECES)),

time: 71.4 us -> 67.9 us (0.951)
  Pallas kernels: 68.5 us -> 64.6 us
    pallas_call x1, Pallas kernels: 68.5 us -> 64.6 us  [fused(): pl.pallas_call(functools.partial(kernel, groups), out_shape=jax.ShapeDtyp...]
where the time goes in v2:
time: 67.9 us; the launch traced here: 66.8 us
  Pallas kernels  64.6 us (95%)
  local copies, waits for them, and re-layouts  2.14 us (3%)
    pallas_call x1, Pallas kernels, fused(): pl.pallas_call(functools.partial(kernel, groups), out_shape=jax.ShapeDtyp...  64.6 us
    unnamed x1, local copies, waits for them, and re-layouts  2.14 us

profile of v2, /device:TPU:13, one launch (start us, length us, event | category | flops | bytes accessed | tf_op | source)
XLA Modules:
  0.0 66.8 jit_solution(6001696935180909703)
XLA Ops:
  0.0 64.6 %shard_map.100 = f32[432,512]{1,0:T(8,128)} custom-call(f32[432,512]{1,0:T(8,128)} %field_ref.1, s32[1,512]{1,0:T(1,128)} %bitcast.5, f32[1,432]{1,0:T(1,128)} %bitcast.6, f32[3,512]{1,0:T(4,128)} %couple_ref.1, f32[1,512]{1,0:T(1,128)} %bitcast.7, f32[16,16]{1,0:T(8,128)} %stencil_ref.1, s32[1,256]{1,0:T(1,128)} %bitcast.9, s32[4,32]{1,0:T(4,128)} %bitcast.8, ...), custom_call_target="tpu_custom_call" | custom-call | tf_op jit(solution)/shard_map/pallas_call | solution.py:431
  64.6 2.1 %copy.12 = f32[432,512]{1,0:T(8,128)} copy(f32[432,512]{1,0:T(8,128)} %shard_map.100) | data formatting | bytes 1769472

commit v3 on v2

--- a/solution.py
+++ b/solution.py
@@ -221,8 +221,7 @@
         for k in range(groups):
             to_home(lax.rem(me + k, groups), p).start()
 
-    for p in range(PIECES):
-        slot_piece(p)
+    slot_piece(0)
 
     for one in loads[:2]:
         one.wait()
@@ -291,10 +290,11 @@
     part = jnp.dot(stencil_ref[...], spread, precision=HIGHEST, preferred_element_type=F32)
     full = lax.dot_general(part, spread, outer, precision=HIGHEST, preferred_element_type=F32)
     same = iota((LANES, LANES), 0) // PTS == iota((LANES, LANES), 1) // PTS
-    operator = jnp.where(same, full, 0.0)
+    op_hi, op_lo = split(jnp.where(same, full, 0.0))
 
     def laplace(x, c):
-        applied = jnp.dot(x, operator, precision=HIGHEST, preferred_element_type=F32)
+        applied = exact_dot(x, op_hi)
+        applied = applied + jnp.dot(x.astype(BF16), op_lo, preferred_element_type=F32)
         return applied * metric_ref[:, c * LANES:(c + 1) * LANES]
 
     def to_left(out, high, n, p):
@@ -322,7 +322,7 @@
         for c in range(2):
             lap1[p, c] = laplace(upd[p, c], c)
         edges(lap1, out1, 0, p)
-        to_left(out1, high1, 0, p).start()
+    slot_piece(1)
 
     col = iota((1, 512), 1)
     point = lax.rem(col, PTS)
@@ -350,6 +350,10 @@
     share = 1.0 / (1.0 + jnp.where((pi == 0) | (pi == NP - 1), 1.0, 0.0)
                    + jnp.where((pj == 0) | (pj == NP - 1), 1.0, 0.0))
 
+    slot_piece(2)
+    for p in range(PIECES):
+        to_left(out1, high1, 0, p).start()
+
     def own_sum(lap, p):
         mine = jnp.concatenate([lap[p, c] for c in range(4)], axis=1)
         return exact_dot(mine, picks[...])
@@ -401,8 +405,8 @@
     first_round(0)
     at_home(2)
     first_round(1)
+    first_round(2)
     second_round(0)
-    first_round(2)
     second_round(1)
     second_round(2)
 

time: 67.9 us -> 66.7 us (0.982); the launches traced: 66.8 us -> 66.5 us
  no operation moved by 1% of the time
where the time goes in v3:
time: 66.7 us; the launch traced here: 66.5 us
  Pallas kernels  64.4 us (97%)
  local copies, waits for them, and re-layouts  2.14 us (3%)
    pallas_call x1, Pallas kernels, fused(): pl.pallas_call(functools.partial(kernel, groups), out_shape=jax.ShapeDtyp...  64.4 us
    unnamed x1, local copies, waits for them, and re-layouts  2.14 us

profile of v3, /device:TPU:13, one launch (start us, length us, event | category | flops | bytes accessed | tf_op | source)
XLA Modules:
  0.0 66.5 jit_solution(2943935316510606672)
XLA Ops:
  0.0 64.4 %shard_map.100 = f32[432,512]{1,0:T(8,128)} custom-call(f32[432,512]{1,0:T(8,128)} %field_ref.1, s32[1,512]{1,0:T(1,128)} %bitcast.5, f32[1,432]{1,0:T(1,128)} %bitcast.6, f32[3,512]{1,0:T(4,128)} %couple_ref.1, f32[1,512]{1,0:T(1,128)} %bitcast.7, f32[16,16]{1,0:T(8,128)} %stencil_ref.1, s32[1,256]{1,0:T(1,128)} %bitcast.9, s32[4,32]{1,0:T(4,128)} %bitcast.8, ...), custom_call_target="tpu_custom_call" | custom-call | tf_op jit(solution)/shard_map/pallas_call | solution.py:435
  64.4 2.1 %copy.12 = f32[432,512]{1,0:T(8,128)} copy(f32[432,512]{1,0:T(8,128)} %shard_map.100) | data formatting | bytes 1769472

commit v4 on v3

--- a/solution.py
+++ b/solution.py
@@ -322,6 +322,7 @@
         for c in range(2):
             lap1[p, c] = laplace(upd[p, c], c)
         edges(lap1, out1, 0, p)
+        to_left(out1, high1, 0, p).start()
     slot_piece(1)
 
     col = iota((1, 512), 1)
@@ -351,8 +352,6 @@
                    + jnp.where((pj == 0) | (pj == NP - 1), 1.0, 0.0))
 
     slot_piece(2)
-    for p in range(PIECES):
-        to_left(out1, high1, 0, p).start()
 
     def own_sum(lap, p):
         mine = jnp.concatenate([lap[p, c] for c in range(4)], axis=1)

time: 66.7 us -> 70.7 us (1.060)
  the two profiles are of different devices: /device:TPU:13 before, /device:TPU:11 now
where the time goes in v4:
time: 70.7 us; the launch traced here: 70.6 us
  Pallas kernels  68.4 us (97%)
  local copies, waits for them, and re-layouts  2.14 us (3%)
    pallas_call x1, Pallas kernels, fused(): pl.pallas_call(functools.partial(kernel, groups), out_shape=jax.ShapeDtyp...  68.4 us
    unnamed x1, local copies, waits for them, and re-layouts  2.14 us

profile of v4, /device:TPU:11, one launch (start us, length us, event | category | flops | bytes accessed | tf_op | source)
XLA Modules:
  0.0 70.6 jit_solution(4072505240582943053)
XLA Ops:
  0.0 68.4 %shard_map.100 = f32[432,512]{1,0:T(8,128)} custom-call(f32[432,512]{1,0:T(8,128)} %field_ref.1, s32[1,512]{1,0:T(1,128)} %bitcast.5, f32[1,432]{1,0:T(1,128)} %bitcast.6, f32[3,512]{1,0:T(4,128)} %couple_ref.1, f32[1,512]{1,0:T(1,128)} %bitcast.7, f32[16,16]{1,0:T(8,128)} %stencil_ref.1, s32[1,256]{1,0:T(1,128)} %bitcast.9, s32[4,32]{1,0:T(4,128)} %bitcast.8, ...), custom_call_target="tpu_custom_call" | custom-call | tf_op jit(solution)/shard_map/pallas_call | solution.py:434
  68.4 2.1 %copy.12 = f32[432,512]{1,0:T(8,128)} copy(f32[432,512]{1,0:T(8,128)} %shard_map.100) | data formatting | bytes 1769472
